TPU v7x, 256 devices: a whole 4x4x8 slice. The times are simulated.
256 devices in a mesh: tm: 8 (over y, core), mp: 4 (over z_lo), tok: 8 (over z_hi, x).
Axes of the slice: x: 4, y: 4, z: 8 (z_hi: 2, z_lo: 4; z = z_hi * 4 + z_lo), core: 2. Of those that a mesh axis runs over, the one named last changes fastest.
Arguments:
- features: bfloat16 [1024, 3584], P('tok'), may hold values from -6 to 6
- spike_mask: int32 [8, 1024, 3584], P('tm', 'tok'), may hold values 0 or 1
- gate_weight: bfloat16 [3584, 7168], P(('tm', 'tok'), 'mp'), may hold values from -0.09375 to 0.09375
- threshold: float32 [7168], P('mp'), may hold values from 0.5 to 2
Outputs:
- rates: float32 [1024, 7168], P('tok', 'mp')
- grad_threshold: float32 [7168], P('mp')
All inputs are finite; a program needn't handle non-finite values. No bound on the sum of `spike_mask` on one device may be relied on, other than what follows from the above.
Results may differ from a plain program's by a relative error of at most 0.00035.
Values may be sent and summed in bfloat16 or wider, within the bound.
No kernel may reach another device: no remote copies, remote signals or barrier semaphores. Data moves between devices by JAX's collectives and lax.ppermute only.
A program may use at most 64 MiB of HBM per device.

v0:
```python
import jax
import jax.numpy as jnp
from jax import lax
from jax.sharding import PartitionSpec as P

SHARP = 2.0


def passed_along(x, axis, by):
    peers = lax.axis_size(axis)
    pairs = [(i, i + by) for i in range(peers) if 0 <= i + by < peers]
    return lax.ppermute(x, axis, pairs)


def on_device(features, spike_mask, gate_weight, threshold):
    steps = lax.axis_size("tm")
    step_index = lax.axis_index("tm")
    tokens_all = features.shape[0] * lax.axis_size("tok")
    rows = features.shape[0]
    width = gate_weight.shape[1]
    driven = jnp.where(spike_mask[0] > 0, features, jnp.zeros_like(features))
    piece = lax.all_gather(gate_weight, ("tm", "tok"), axis=0, tiled=True)
    student = jnp.dot(driven, piece, preferred_element_type=jnp.float32)
    teacher = jnp.dot(features, piece, preferred_element_type=jnp.float32)
    current = 2.0 * student
    target = jax.nn.silu(teacher)
    blocks = 1
    size = rows // blocks
    turns = steps + blocks - 1

    def forward_turn(turn, carry):
        incoming, spikes = carry
        block = turn - step_index
        active = (block >= 0) & (block < blocks)
        rising = incoming + current
        fired = jax.nn.sigmoid(SHARP * (rising - threshold))
        leaving = rising - threshold * fired
        older = spikes
        spikes = jnp.where(active, fired, older)
        passed = passed_along(leaving, "tm", 1)
        return (passed, spikes)

    block_zero = jnp.zeros((size, width), jnp.float32)
    unused, spikes = lax.fori_loop(
        0, turns, forward_turn, (block_zero, jnp.zeros((rows, width), jnp.float32))
    )
    total = lax.psum(spikes, "tm")
    rates = threshold * total / steps
    error = (rates - target) / tokens_all

    def backward_turn(turn, carry):
        incoming, grad_sum = carry
        block = turn - (steps - 1 - step_index)
        active = (block >= 0) & (block < blocks)
        dspike = error * threshold / steps - threshold * incoming
        dwide = dspike * SHARP * spikes * (1.0 - spikes)
        term = jnp.sum(-dwide - spikes * incoming + error * spikes / steps, axis=0)
        grad_sum = grad_sum + jnp.where(active, term, jnp.zeros_like(term))
        passed = passed_along((incoming + dwide).astype(jnp.bfloat16), "tm", -1).astype(jnp.float32)
        return (passed, grad_sum)

    unused_cot, grad_local = lax.fori_loop(
        0, turns, backward_turn, (block_zero, jnp.zeros((width,), jnp.float32))
    )
    grad_threshold = lax.psum(grad_local, ("tm", "tok"))
    return (rates, grad_threshold)


def solution(mesh):
    return jax.shard_map(
        on_device,
        mesh=mesh,
        in_specs=(P("tok", None), P("tm", "tok", None), P(("tm", "tok"), "mp"), P("mp")),
        out_specs=(P("tok", "mp"), P("mp")),
        check_vma=False,
    )
```

profile of v0, /device:TPU:32, one launch (start us, length us, event | category | flops | bytes accessed | tf_op | source)
XLA Modules:
  0.0 676.2 jit_solution(10581541776726929995)
XLA Ops:
  8.0 140.1 %all-gather.2.cloned.1.call-done = bf16[3584,1792]{1,0:T(8,128)(2,1)} async-done(((bf16[56,1792]{1,0:T(8,128)(2,1)}), bf16[3584,1792]{1,0:T(8,128)(2,1)}) %all-gather.2.cloned.1.call-update) | async-done | bytes 12845072 | tf_op jit(solution)/shard_map/all_gather | solution.py:22
  148.0 7.4 %convolution_multiply_fusion = f32[128,1792]{1,0:T(8,128)S(1)} fusion(bf16[3584,1792]{1,0:T(8,128)(2,1)} %all-gather.2.cloned.1.call-done, bf16[128,3584]{1,0:T(8,128)(2,1)} %param.8, s32[1,128,3584]{2,1,0:T(8,128)} %param.9), kind=kOutput, calls=%fused_computation.8 | convolution fusion | flops 1645314048 | bytes 16515072 | tf_op jit(solution)/shard_map/dot_general | solution.py:23
  155.5 120.2 %while.34 = (s32[]{:T(128)}, f32[128,1792]{1,0:T(8,128)S(1)}, f32[128,1792]{1,0:T(8,128)S(1)}, f32[128,1792]{1,0:T(8,128)S(1)}, f32[1792]{0:T(1024)S(1)}, /*index=5*/s32[]{:T(128)}, s32[]{:T(128)}, s32[]{:T(128)}) while((s32[]{:T(128)}, f32[128,1792]{1,0:T(8,128)S(1)}, f32[128,1792]{1,0:T(8,128)S(1)}, f32[128,1792]{1,0:T(8,128)S(1)}, ...), condition=%wide.region_1.2_spmd.clone, body=%wide.region_0.1_spmd.clone.sunk | while | flops 2293767 | bytes 8264873 | solution.py:44
  157.1 2.2 collective-permute-start
  159.3 2.2 collective-permute-done
  163.1 11.6 %collective-permute-start = (f32[128,1792]{1,0:T(8,128)}, f32[128,1792]{1,0:T(8,128)S(1)}, u32[]{:S(2)}, u32[]{:S(2)}) collective-permute-start(f32[128,1792]{1,0:T(8,128)} %get-tuple-element.455), channel_id=1, source_target_pairs={{0,32},{32,64},{64,96},{96,128},{128,160},{160,192},{192,224},{1,3... | collective-permute-start | bytes 2752520 | tf_op jit(solution)/shard_map/while/body/eval_jaxpr/ppermute | solution.py:12
  174.7 2.2 collective-permute-done
  178.4 12.7 %collective-permute-start = (f32[128,1792]{1,0:T(8,128)}, f32[128,1792]{1,0:T(8,128)S(1)}, u32[]{:S(2)}, u32[]{:S(2)}) collective-permute-start(f32[128,1792]{1,0:T(8,128)} %get-tuple-element.455), channel_id=1, source_target_pairs={{0,32},{32,64},{64,96},{96,128},{128,160},{160,192},{192,224},{1,3... | collective-permute-start | bytes 2752520 | tf_op jit(solution)/shard_map/while/body/eval_jaxpr/ppermute | solution.py:12
  191.1 2.2 collective-permute-done
  194.9 12.7 %collective-permute-start = (f32[128,1792]{1,0:T(8,128)}, f32[128,1792]{1,0:T(8,128)S(1)}, u32[]{:S(2)}, u32[]{:S(2)}) collective-permute-start(f32[128,1792]{1,0:T(8,128)} %get-tuple-element.455), channel_id=1, source_target_pairs={{0,32},{32,64},{64,96},{96,128},{128,160},{160,192},{192,224},{1,3... | collective-permute-start | bytes 2752520 | tf_op jit(solution)/shard_map/while/body/eval_jaxpr/ppermute | solution.py:12
  207.6 2.2 collective-permute-done
  211.4 12.7 %collective-permute-start = (f32[128,1792]{1,0:T(8,128)}, f32[128,1792]{1,0:T(8,128)S(1)}, u32[]{:S(2)}, u32[]{:S(2)}) collective-permute-start(f32[128,1792]{1,0:T(8,128)} %get-tuple-element.455), channel_id=1, source_target_pairs={{0,32},{32,64},{64,96},{96,128},{128,160},{160,192},{192,224},{1,3... | collective-permute-start | bytes 2752520 | tf_op jit(solution)/shard_map/while/body/eval_jaxpr/ppermute | solution.py:12
  224.0 2.2 collective-permute-done
  227.8 12.7 %collective-permute-start = (f32[128,1792]{1,0:T(8,128)}, f32[128,1792]{1,0:T(8,128)S(1)}, u32[]{:S(2)}, u32[]{:S(2)}) collective-permute-start(f32[128,1792]{1,0:T(8,128)} %get-tuple-element.455), channel_id=1, source_target_pairs={{0,32},{32,64},{64,96},{96,128},{128,160},{160,192},{192,224},{1,3... | collective-permute-start | bytes 2752520 | tf_op jit(solution)/shard_map/while/body/eval_jaxpr/ppermute | solution.py:12
  240.5 2.2 collective-permute-done
  244.3 12.7 %collective-permute-start = (f32[128,1792]{1,0:T(8,128)}, f32[128,1792]{1,0:T(8,128)S(1)}, u32[]{:S(2)}, u32[]{:S(2)}) collective-permute-start(f32[128,1792]{1,0:T(8,128)} %get-tuple-element.455), channel_id=1, source_target_pairs={{0,32},{32,64},{64,96},{96,128},{128,160},{160,192},{192,224},{1,3... | collective-permute-start | bytes 2752520 | tf_op jit(solution)/shard_map/while/body/eval_jaxpr/ppermute | solution.py:12
  256.9 2.2 collective-permute-done
  260.7 12.7 %collective-permute-start = (f32[128,1792]{1,0:T(8,128)}, f32[128,1792]{1,0:T(8,128)S(1)}, u32[]{:S(2)}, u32[]{:S(2)}) collective-permute-start(f32[128,1792]{1,0:T(8,128)} %get-tuple-element.455), channel_id=1, source_target_pairs={{0,32},{32,64},{64,96},{96,128},{128,160},{160,192},{192,224},{1,3... | collective-permute-start | bytes 2752520 | tf_op jit(solution)/shard_map/while/body/eval_jaxpr/ppermute | solution.py:12
  273.4 2.2 collective-permute-done
  276.7 74.4 %all-reduce.2.cloned.1.call-done = f32[128,1792]{1,0:T(8,128)} async-done(((f32[128,1792]{1,0:T(8,128)}), f32[128,1792]{1,0:T(8,128)}) %all-reduce.2.cloned.1.call-update) | async-done | bytes 917520 | tf_op jit(solution)/shard_map/psum | solution.py:47
  351.1 8.4 %fusion.4 = (f32[128,1792]{1,0:T(8,128)S(1)}, f32[128,1792]{1,0:T(8,128)S(1)}, f32[128,1792]{1,0:T(8,128)}) fusion(f32[128,1792]{1,0:T(8,128)} %copy-done, f32[128,1792]{1,0:T(8,128)} %all-reduce.2.cloned.1.call-done, f32[1792]{0:T(1024)S(1)} %get-tuple-element.528, bf16[128,3584]{1,0:T(8,128)(2,1)} %param.8, ...), kind=kOutput, calls=%fused_computation.16 | convolution fusion | flops 1646231552 | bytes 18357248 | tf_op jit(solution)/shard_map/dot_general | solution.py:24
  359.4 99.1 %while.35 = (s32[]{:T(128)}, f32[128,1792]{1,0:T(8,128)}, f32[1792]{0:T(1024)S(1)}, f32[1792]{0:T(1024)S(1)}, f32[128,1792]{1,0:T(8,128)S(1)}, /*index=5*/f32[12...) while((s32[]{:T(128)}, f32[128,1792]{1,0:T(8,128)}, ...), condition=%wide.region_5.6_spmd.clone, body=%wide.region_3.5_spmd.clone.sunk | while | flops 4132359 | bytes 7376058 | solution.py:62
  361.3 2.5 collective-permute-done.1
  363.8 2.0 convert_element_type.22
  368.8 5.9 collective-permute-done.1
  379.8 8.6 %collective-permute-done.1 = bf16[128,1792]{1,0:T(8,128)(2,1)} collective-permute-done((bf16[128,1792]{1,0:T(8,128)(2,1)S(1)}, bf16[128,1792]{1,0:T(8,128)(2,1)}, u32[]{:S(2)}, u32[]{:S(2)}) %collective-permute-start.1) | collective-permute-done | bytes 458784 | tf_op jit(solution)/shard_map/while/body/eval_jaxpr/ppermute | solution.py:12
  393.4 8.6 %collective-permute-done.1 = bf16[128,1792]{1,0:T(8,128)(2,1)} collective-permute-done((bf16[128,1792]{1,0:T(8,128)(2,1)S(1)}, bf16[128,1792]{1,0:T(8,128)(2,1)}, u32[]{:S(2)}, u32[]{:S(2)}) %collective-permute-start.1) | collective-permute-done | bytes 458784 | tf_op jit(solution)/shard_map/while/body/eval_jaxpr/ppermute | solution.py:12
  407.0 8.6 %collective-permute-done.1 = bf16[128,1792]{1,0:T(8,128)(2,1)} collective-permute-done((bf16[128,1792]{1,0:T(8,128)(2,1)S(1)}, bf16[128,1792]{1,0:T(8,128)(2,1)}, u32[]{:S(2)}, u32[]{:S(2)}) %collective-permute-start.1) | collective-permute-done | bytes 458784 | tf_op jit(solution)/shard_map/while/body/eval_jaxpr/ppermute | solution.py:12
  420.7 8.6 %collective-permute-done.1 = bf16[128,1792]{1,0:T(8,128)(2,1)} collective-permute-done((bf16[128,1792]{1,0:T(8,128)(2,1)S(1)}, bf16[128,1792]{1,0:T(8,128)(2,1)}, u32[]{:S(2)}, u32[]{:S(2)}) %collective-permute-start.1) | collective-permute-done | bytes 458784 | tf_op jit(solution)/shard_map/while/body/eval_jaxpr/ppermute | solution.py:12
  434.3 8.6 %collective-permute-done.1 = bf16[128,1792]{1,0:T(8,128)(2,1)} collective-permute-done((bf16[128,1792]{1,0:T(8,128)(2,1)S(1)}, bf16[128,1792]{1,0:T(8,128)(2,1)}, u32[]{:S(2)}, u32[]{:S(2)}) %collective-permute-start.1) | collective-permute-done | bytes 458784 | tf_op jit(solution)/shard_map/while/body/eval_jaxpr/ppermute | solution.py:12
  447.9 8.6 %collective-permute-done.1 = bf16[128,1792]{1,0:T(8,128)(2,1)} collective-permute-done((bf16[128,1792]{1,0:T(8,128)(2,1)S(1)}, bf16[128,1792]{1,0:T(8,128)(2,1)}, u32[]{:S(2)}, u32[]{:S(2)}) %collective-permute-start.1) | collective-permute-done | bytes 458784 | tf_op jit(solution)/shard_map/while/body/eval_jaxpr/ppermute | solution.py:12
  458.5 210.8 %psum.15 = f32[1792]{0:T(1024)} all-reduce(f32[1792]{0:T(1024)S(1)} %get-tuple-element.289), channel_id=1, replica_groups=mesh['tm'=8,'mp'=4,'tok'=8] {'tm','tok'}, use_global_device_ids=true, to_apply=%region_6.7 | all-reduce | flops 1792 | bytes 14336 | tf_op jit(solution)/shard_map/psum | solution.py:65
  (53 shorter events, 51.1 us)
Async XLA Ops:
  7.2 140.9 %all-gather.2.cloned.1.call-start = ((), (), s32[]{:S(2)}) async-start(), calls=%async_computation | async-start | bytes 13045760 | tf_op jit(solution)/shard_map/all_gather | solution.py:22
  7.9 343.2 %all-reduce.2.cloned.1.call-start = ((), (), s32[]{:S(2)}) async-start(), calls=%async_computation.1 | async-start | bytes 1835008 | tf_op jit(solution)/shard_map/psum | solution.py:47
  8.0 147.5 %copy-start.2 = (f32[1792]{0:T(1024)S(1)}, f32[1792]{0:T(1024)}, u32[]{:S(2)}) copy-start(f32[1792]{0:T(1024)} %param.11) | copy-start | bytes 21508
  157.1 4.5 collective-permute-start
  163.1 13.8 %collective-permute-start = (f32[128,1792]{1,0:T(8,128)}, f32[128,1792]{1,0:T(8,128)S(1)}, u32[]{:S(2)}, u32[]{:S(2)}) collective-permute-start(f32[128,1792]{1,0:T(8,128)} %get-tuple-element.455), channel_id=1, source_target_pairs={{0,32},{32,64},{64,96},{96,128},{128,160},{160,192},{192,224},{1,3... | collective-permute-start | bytes 2752520 | tf_op jit(solution)/shard_map/while/body/eval_jaxpr/ppermute | solution.py:12
  178.4 14.9 %collective-permute-start = (f32[128,1792]{1,0:T(8,128)}, f32[128,1792]{1,0:T(8,128)S(1)}, u32[]{:S(2)}, u32[]{:S(2)}) collective-permute-start(f32[128,1792]{1,0:T(8,128)} %get-tuple-element.455), channel_id=1, source_target_pairs={{0,32},{32,64},{64,96},{96,128},{128,160},{160,192},{192,224},{1,3... | collective-permute-start | bytes 2752520 | tf_op jit(solution)/shard_map/while/body/eval_jaxpr/ppermute | solution.py:12
  194.9 14.9 %collective-permute-start = (f32[128,1792]{1,0:T(8,128)}, f32[128,1792]{1,0:T(8,128)S(1)}, u32[]{:S(2)}, u32[]{:S(2)}) collective-permute-start(f32[128,1792]{1,0:T(8,128)} %get-tuple-element.455), channel_id=1, source_target_pairs={{0,32},{32,64},{64,96},{96,128},{128,160},{160,192},{192,224},{1,3... | collective-permute-start | bytes 2752520 | tf_op jit(solution)/shard_map/while/body/eval_jaxpr/ppermute | solution.py:12
  211.4 14.9 %collective-permute-start = (f32[128,1792]{1,0:T(8,128)}, f32[128,1792]{1,0:T(8,128)S(1)}, u32[]{:S(2)}, u32[]{:S(2)}) collective-permute-start(f32[128,1792]{1,0:T(8,128)} %get-tuple-element.455), channel_id=1, source_target_pairs={{0,32},{32,64},{64,96},{96,128},{128,160},{160,192},{192,224},{1,3... | collective-permute-start | bytes 2752520 | tf_op jit(solution)/shard_map/while/body/eval_jaxpr/ppermute | solution.py:12
  227.8 14.9 %collective-permute-start = (f32[128,1792]{1,0:T(8,128)}, f32[128,1792]{1,0:T(8,128)S(1)}, u32[]{:S(2)}, u32[]{:S(2)}) collective-permute-start(f32[128,1792]{1,0:T(8,128)} %get-tuple-element.455), channel_id=1, source_target_pairs={{0,32},{32,64},{64,96},{96,128},{128,160},{160,192},{192,224},{1,3... | collective-permute-start | bytes 2752520 | tf_op jit(solution)/shard_map/while/body/eval_jaxpr/ppermute | solution.py:12
  244.3 14.9 %collective-permute-start = (f32[128,1792]{1,0:T(8,128)}, f32[128,1792]{1,0:T(8,128)S(1)}, u32[]{:S(2)}, u32[]{:S(2)}) collective-permute-start(f32[128,1792]{1,0:T(8,128)} %get-tuple-element.455), channel_id=1, source_target_pairs={{0,32},{32,64},{64,96},{96,128},{128,160},{160,192},{192,224},{1,3... | collective-permute-start | bytes 2752520 | tf_op jit(solution)/shard_map/while/body/eval_jaxpr/ppermute | solution.py:12
  260.7 14.9 %collective-permute-start = (f32[128,1792]{1,0:T(8,128)}, f32[128,1792]{1,0:T(8,128)S(1)}, u32[]{:S(2)}, u32[]{:S(2)}) collective-permute-start(f32[128,1792]{1,0:T(8,128)} %get-tuple-element.455), channel_id=1, source_target_pairs={{0,32},{32,64},{64,96},{96,128},{128,160},{160,192},{192,224},{1,3... | collective-permute-start | bytes 2752520 | tf_op jit(solution)/shard_map/while/body/eval_jaxpr/ppermute | solution.py:12
  275.6 1.0 copy-start
  276.7 82.8 %copy-start.1 = (f32[128,1792]{1,0:T(8,128)S(1)}, f32[128,1792]{1,0:T(8,128)}, u32[]{:S(2)}) copy-start(f32[128,1792]{1,0:T(8,128)} %copy-done) | copy-start | bytes 2752516
  360.0 3.8 collective-permute-start.1
  367.5 7.2 %collective-permute-start.1 = (bf16[128,1792]{1,0:T(8,128)(2,1)S(1)}, bf16[128,1792]{1,0:T(8,128)(2,1)}, u32[]{:S(2)}, u32[]{:S(2)}) collective-permute-start(bf16[128,1792]{1,0:T(8,128)(2,1)S(1)} %get-tuple-element.465), channel_id=1, source_target_pairs={{32,0},{64,32},{96,64},{128,96},{160,128},{192,160},{224,192},{33,... | collective-permute-start | bytes 1376264 | tf_op jit(solution)/shard_map/while/body/eval_jaxpr/ppermute | solution.py:12
  378.5 9.9 %collective-permute-start.1 = (bf16[128,1792]{1,0:T(8,128)(2,1)S(1)}, bf16[128,1792]{1,0:T(8,128)(2,1)}, u32[]{:S(2)}, u32[]{:S(2)}) collective-permute-start(bf16[128,1792]{1,0:T(8,128)(2,1)S(1)} %get-tuple-element.465), channel_id=1, source_target_pairs={{32,0},{64,32},{96,64},{128,96},{160,128},{192,160},{224,192},{33,... | collective-permute-start | bytes 1376264 | tf_op jit(solution)/shard_map/while/body/eval_jaxpr/ppermute | solution.py:12
  392.1 9.9 %collective-permute-start.1 = (bf16[128,1792]{1,0:T(8,128)(2,1)S(1)}, bf16[128,1792]{1,0:T(8,128)(2,1)}, u32[]{:S(2)}, u32[]{:S(2)}) collective-permute-start(bf16[128,1792]{1,0:T(8,128)(2,1)S(1)} %get-tuple-element.465), channel_id=1, source_target_pairs={{32,0},{64,32},{96,64},{128,96},{160,128},{192,160},{224,192},{33,... | collective-permute-start | bytes 1376264 | tf_op jit(solution)/shard_map/while/body/eval_jaxpr/ppermute | solution.py:12
  405.7 9.9 %collective-permute-start.1 = (bf16[128,1792]{1,0:T(8,128)(2,1)S(1)}, bf16[128,1792]{1,0:T(8,128)(2,1)}, u32[]{:S(2)}, u32[]{:S(2)}) collective-permute-start(bf16[128,1792]{1,0:T(8,128)(2,1)S(1)} %get-tuple-element.465), channel_id=1, source_target_pairs={{32,0},{64,32},{96,64},{128,96},{160,128},{192,160},{224,192},{33,... | collective-permute-start | bytes 1376264 | tf_op jit(solution)/shard_map/while/body/eval_jaxpr/ppermute | solution.py:12
  419.3 9.9 %collective-permute-start.1 = (bf16[128,1792]{1,0:T(8,128)(2,1)S(1)}, bf16[128,1792]{1,0:T(8,128)(2,1)}, u32[]{:S(2)}, u32[]{:S(2)}) collective-permute-start(bf16[128,1792]{1,0:T(8,128)(2,1)S(1)} %get-tuple-element.465), channel_id=1, source_target_pairs={{32,0},{64,32},{96,64},{128,96},{160,128},{192,160},{224,192},{33,... | collective-permute-start | bytes 1376264 | tf_op jit(solution)/shard_map/while/body/eval_jaxpr/ppermute | solution.py:12
  433.0 9.9 %collective-permute-start.1 = (bf16[128,1792]{1,0:T(8,128)(2,1)S(1)}, bf16[128,1792]{1,0:T(8,128)(2,1)}, u32[]{:S(2)}, u32[]{:S(2)}) collective-permute-start(bf16[128,1792]{1,0:T(8,128)(2,1)S(1)} %get-tuple-element.465), channel_id=1, source_target_pairs={{32,0},{64,32},{96,64},{128,96},{160,128},{192,160},{224,192},{33,... | collective-permute-start | bytes 1376264 | tf_op jit(solution)/shard_map/while/body/eval_jaxpr/ppermute | solution.py:12
  446.6 9.9 %collective-permute-start.1 = (bf16[128,1792]{1,0:T(8,128)(2,1)S(1)}, bf16[128,1792]{1,0:T(8,128)(2,1)}, u32[]{:S(2)}, u32[]{:S(2)}) collective-permute-start(bf16[128,1792]{1,0:T(8,128)(2,1)S(1)} %get-tuple-element.465), channel_id=1, source_target_pairs={{32,0},{64,32},{96,64},{128,96},{160,128},{192,160},{224,192},{33,... | collective-permute-start | bytes 1376264 | tf_op jit(solution)/shard_map/while/body/eval_jaxpr/ppermute | solution.py:12
Sparse Core Ops, SparseCore 0:
  11.7 136.3 all-gather.1
  276.8 74.2 all-reduce.1
where the time goes:
time: 677 us; the launch traced here: 676 us
  waiting for transfers between devices  293 us (43%)
  blocking collectives  211 us (31%)
  starting transfers between devices  100 us (15%)
  other arithmetic  41 us (6%)
  matrix products  15.7 us (2%)
  between operations  14.1 us (2%)
    psum x1, blocking collectives, on_device(): grad_threshold = lax.psum(grad_local, ('tm', 'tok'))  211 us
    all_gather x1, waiting for transfers between devices, on_device(): piece = lax.all_gather(gate_weight, ('tm', 'tok'), axis=0, tiled=True)  140 us
    ppermute x16, starting transfers between devices, passed_along(): return lax.ppermute(x, axis, pairs)  100 us
    ppermute x16, waiting for transfers between devices, passed_along(): return lax.ppermute(x, axis, pairs)  77.7 us
    psum x1, waiting for transfers between devices, on_device(): total = lax.psum(spikes, 'tm')  74.4 us
    convert_element_type x8, other arithmetic, backward_turn(): passed_along((incoming + dwide).astype(jnp.bfloat16), 'tm', -1)  16.3 us
  transfers between devices with their start and end apart: 18, of which 18 were waited for; matrix products, arithmetic and copies ran while one was open for 0% of the time, Pallas kernels for 0%

commit v1 on v0

--- a/solution.py
+++ b/solution.py
@@ -2,6 +2,7 @@
 import jax.numpy as jnp
 from jax import lax
 from jax.sharding import PartitionSpec as P
+from jax.lax import psum
 
 SHARP = 2.0
 
@@ -62,7 +63,7 @@
     unused_cot, grad_local = lax.fori_loop(
         0, turns, backward_turn, (block_zero, jnp.zeros((width,), jnp.float32))
     )
-    grad_threshold = lax.psum(grad_local, ("tm", "tok"))
+    grad_threshold = psum(psum(grad_local, "tm"), "tok")
     return (rates, grad_threshold)
 
 

time: 677 us -> 517 us (0.76)
  blocking collectives: 211 us -> 50.8 us
    psum x1 -> x2, blocking collectives: 211 us -> 50.8 us  [on_device(): grad_threshold = psum(psum(grad_local, 'tm'), 'tok')]
where the time goes in v1:
time: 517 us; the launch traced here: 516 us
  waiting for transfers between devices  293 us (57%)
  starting transfers between devices  100 us (19%)
  blocking collectives  50.8 us (10%)
  other arithmetic  40.8 us (8%)
  matrix products  15.7 us (3%)
  between operations  14.1 us (3%)
    all_gather x1, waiting for transfers between devices, on_device(): piece = lax.all_gather(gate_weight, ('tm', 'tok'), axis=0, tiled=True)  140 us
    ppermute x16, starting transfers between devices, passed_along(): return lax.ppermute(x, axis, pairs)  100 us
    ppermute x16, waiting for transfers between devices, passed_along(): return lax.ppermute(x, axis, pairs)  77.7 us
    psum x1, waiting for transfers between devices, on_device(): total = lax.psum(spikes, 'tm')  74.4 us
    psum x2, blocking collectives, on_device(): grad_threshold = psum(psum(grad_local, 'tm'), 'tok')  50.8 us
    convert_element_type x8, other arithmetic, backward_turn(): passed_along((incoming + dwide).astype(jnp.bfloat16), 'tm', -1)  16.1 us
    select_n x8, other arithmetic, forward_turn(): spikes = jnp.where(active, fired, older)  12.4 us
    reduce_sum x8, other arithmetic, backward_turn(): term = jnp.sum(-dwide - spikes * incoming + error * spikes / steps, axis=0)  12.3 us
  transfers between devices with their start and end apart: 18, of which 18 were waited for; matrix products, arithmetic and copies ran while one was open for 0% of the time, Pallas kernels for 0%

profile of v1, /device:TPU:32, one launch (start us, length us, event | category | flops | bytes accessed | tf_op | source)
XLA Modules:
  0.0 515.9 jit_solution(5008851999693369346)
XLA Ops:
  8.0 140.1 %all-gather.2.cloned.1.call-done = bf16[3584,1792]{1,0:T(8,128)(2,1)} async-done(((bf16[56,1792]{1,0:T(8,128)(2,1)}), bf16[3584,1792]{1,0:T(8,128)(2,1)}) %all-gather.2.cloned.1.call-update) | async-done | bytes 12845072 | tf_op jit(solution)/shard_map/all_gather | solution.py:23
  148.0 7.4 %convolution_multiply_fusion = f32[128,1792]{1,0:T(8,128)S(1)} fusion(bf16[3584,1792]{1,0:T(8,128)(2,1)} %all-gather.2.cloned.1.call-done, bf16[128,3584]{1,0:T(8,128)(2,1)} %param.8, s32[1,128,3584]{2,1,0:T(8,128)} %param.9), kind=kOutput, calls=%fused_computation.8 | convolution fusion | flops 1645314048 | bytes 16515072 | tf_op jit(solution)/shard_map/dot_general | solution.py:24
  155.5 120.2 %while.34 = (s32[]{:T(128)}, f32[128,1792]{1,0:T(8,128)S(1)}, f32[128,1792]{1,0:T(8,128)S(1)}, f32[128,1792]{1,0:T(8,128)S(1)}, f32[1792]{0:T(1024)S(1)}, /*index=5*/s32[]{:T(128)}, s32[]{:T(128)}, s32[]{:T(128)}) while((s32[]{:T(128)}, f32[128,1792]{1,0:T(8,128)S(1)}, f32[128,1792]{1,0:T(8,128)S(1)}, f32[128,1792]{1,0:T(8,128)S(1)}, ...), condition=%wide.region_1.2_spmd.clone, body=%wide.region_0.1_spmd.clone.sunk | while | flops 2293767 | bytes 8264873 | solution.py:45
  157.1 2.2 collective-permute-start
  159.3 2.2 collective-permute-done
  163.1 11.6 %collective-permute-start = (f32[128,1792]{1,0:T(8,128)}, f32[128,1792]{1,0:T(8,128)S(1)}, u32[]{:S(2)}, u32[]{:S(2)}) collective-permute-start(f32[128,1792]{1,0:T(8,128)} %get-tuple-element.455), channel_id=1, source_target_pairs={{0,32},{32,64},{64,96},{96,128},{128,160},{160,192},{192,224},{1,3... | collective-permute-start | bytes 2752520 | tf_op jit(solution)/shard_map/while/body/eval_jaxpr/ppermute | solution.py:13
  174.7 2.2 collective-permute-done
  178.4 12.7 %collective-permute-start = (f32[128,1792]{1,0:T(8,128)}, f32[128,1792]{1,0:T(8,128)S(1)}, u32[]{:S(2)}, u32[]{:S(2)}) collective-permute-start(f32[128,1792]{1,0:T(8,128)} %get-tuple-element.455), channel_id=1, source_target_pairs={{0,32},{32,64},{64,96},{96,128},{128,160},{160,192},{192,224},{1,3... | collective-permute-start | bytes 2752520 | tf_op jit(solution)/shard_map/while/body/eval_jaxpr/ppermute | solution.py:13
  191.1 2.2 collective-permute-done
  194.9 12.7 %collective-permute-start = (f32[128,1792]{1,0:T(8,128)}, f32[128,1792]{1,0:T(8,128)S(1)}, u32[]{:S(2)}, u32[]{:S(2)}) collective-permute-start(f32[128,1792]{1,0:T(8,128)} %get-tuple-element.455), channel_id=1, source_target_pairs={{0,32},{32,64},{64,96},{96,128},{128,160},{160,192},{192,224},{1,3... | collective-permute-start | bytes 2752520 | tf_op jit(solution)/shard_map/while/body/eval_jaxpr/ppermute | solution.py:13
  207.6 2.2 collective-permute-done
  211.4 12.7 %collective-permute-start = (f32[128,1792]{1,0:T(8,128)}, f32[128,1792]{1,0:T(8,128)S(1)}, u32[]{:S(2)}, u32[]{:S(2)}) collective-permute-start(f32[128,1792]{1,0:T(8,128)} %get-tuple-element.455), channel_id=1, source_target_pairs={{0,32},{32,64},{64,96},{96,128},{128,160},{160,192},{192,224},{1,3... | collective-permute-start | bytes 2752520 | tf_op jit(solution)/shard_map/while/body/eval_jaxpr/ppermute | solution.py:13
  224.0 2.2 collective-permute-done
  227.8 12.7 %collective-permute-start = (f32[128,1792]{1,0:T(8,128)}, f32[128,1792]{1,0:T(8,128)S(1)}, u32[]{:S(2)}, u32[]{:S(2)}) collective-permute-start(f32[128,1792]{1,0:T(8,128)} %get-tuple-element.455), channel_id=1, source_target_pairs={{0,32},{32,64},{64,96},{96,128},{128,160},{160,192},{192,224},{1,3... | collective-permute-start | bytes 2752520 | tf_op jit(solution)/shard_map/while/body/eval_jaxpr/ppermute | solution.py:13
  240.5 2.2 collective-permute-done
  244.3 12.7 %collective-permute-start = (f32[128,1792]{1,0:T(8,128)}, f32[128,1792]{1,0:T(8,128)S(1)}, u32[]{:S(2)}, u32[]{:S(2)}) collective-permute-start(f32[128,1792]{1,0:T(8,128)} %get-tuple-element.455), channel_id=1, source_target_pairs={{0,32},{32,64},{64,96},{96,128},{128,160},{160,192},{192,224},{1,3... | collective-permute-start | bytes 2752520 | tf_op jit(solution)/shard_map/while/body/eval_jaxpr/ppermute | solution.py:13
  256.9 2.2 collective-permute-done
  260.7 12.7 %collective-permute-start = (f32[128,1792]{1,0:T(8,128)}, f32[128,1792]{1,0:T(8,128)S(1)}, u32[]{:S(2)}, u32[]{:S(2)}) collective-permute-start(f32[128,1792]{1,0:T(8,128)} %get-tuple-element.455), channel_id=1, source_target_pairs={{0,32},{32,64},{64,96},{96,128},{128,160},{160,192},{192,224},{1,3... | collective-permute-start | bytes 2752520 | tf_op jit(solution)/shard_map/while/body/eval_jaxpr/ppermute | solution.py:13
  273.4 2.2 collective-permute-done
  276.7 74.4 %all-reduce.2.cloned.1.call-done = f32[128,1792]{1,0:T(8,128)} async-done(((f32[128,1792]{1,0:T(8,128)}), f32[128,1792]{1,0:T(8,128)}) %all-reduce.2.cloned.1.call-update) | async-done | bytes 917520 | tf_op jit(solution)/shard_map/psum | solution.py:48
  351.1 8.4 %fusion.4 = (f32[128,1792]{1,0:T(8,128)S(1)}, f32[128,1792]{1,0:T(8,128)S(1)}, f32[128,1792]{1,0:T(8,128)}) fusion(f32[128,1792]{1,0:T(8,128)} %copy-done, f32[128,1792]{1,0:T(8,128)} %all-reduce.2.cloned.1.call-done, f32[1792]{0:T(1024)S(1)} %get-tuple-element.528, bf16[128,3584]{1,0:T(8,128)(2,1)} %param.8, ...), kind=kOutput, calls=%fused_computation.16 | convolution fusion | flops 1646231552 | bytes 18357248 | tf_op jit(solution)/shard_map/dot_general | solution.py:25
  359.5 98.9 %while.35 = (s32[]{:T(128)}, f32[128,1792]{1,0:T(8,128)}, f32[1792]{0:T(1024)S(1)}, f32[1792]{0:T(1024)S(1)}, f32[128,1792]{1,0:T(8,128)S(1)}, /*index=5*/f32[12...) while((s32[]{:T(128)}, f32[128,1792]{1,0:T(8,128)}, ...), condition=%wide.region_5.6_spmd.clone, body=%wide.region_3.5_spmd.clone.sunk | while | flops 4132359 | bytes 7376058 | solution.py:63
  361.3 2.5 collective-permute-done.1
  368.8 5.9 %collective-permute-done.1 = bf16[128,1792]{1,0:T(8,128)(2,1)} collective-permute-done((bf16[128,1792]{1,0:T(8,128)(2,1)S(1)}, bf16[128,1792]{1,0:T(8,128)(2,1)}, u32[]{:S(2)}, u32[]{:S(2)}) %collective-permute-start.1) | collective-permute-done | bytes 458784 | tf_op jit(solution)/shard_map/while/body/eval_jaxpr/ppermute | solution.py:13
  379.8 8.6 %collective-permute-done.1 = bf16[128,1792]{1,0:T(8,128)(2,1)} collective-permute-done((bf16[128,1792]{1,0:T(8,128)(2,1)S(1)}, bf16[128,1792]{1,0:T(8,128)(2,1)}, u32[]{:S(2)}, u32[]{:S(2)}) %collective-permute-start.1) | collective-permute-done | bytes 458784 | tf_op jit(solution)/shard_map/while/body/eval_jaxpr/ppermute | solution.py:13
  393.4 8.6 %collective-permute-done.1 = bf16[128,1792]{1,0:T(8,128)(2,1)} collective-permute-done((bf16[128,1792]{1,0:T(8,128)(2,1)S(1)}, bf16[128,1792]{1,0:T(8,128)(2,1)}, u32[]{:S(2)}, u32[]{:S(2)}) %collective-permute-start.1) | collective-permute-done | bytes 458784 | tf_op jit(solution)/shard_map/while/body/eval_jaxpr/ppermute | solution.py:13
  407.0 8.6 %collective-permute-done.1 = bf16[128,1792]{1,0:T(8,128)(2,1)} collective-permute-done((bf16[128,1792]{1,0:T(8,128)(2,1)S(1)}, bf16[128,1792]{1,0:T(8,128)(2,1)}, u32[]{:S(2)}, u32[]{:S(2)}) %collective-permute-start.1) | collective-permute-done | bytes 458784 | tf_op jit(solution)/shard_map/while/body/eval_jaxpr/ppermute | solution.py:13
  420.6 8.6 %collective-permute-done.1 = bf16[128,1792]{1,0:T(8,128)(2,1)} collective-permute-done((bf16[128,1792]{1,0:T(8,128)(2,1)S(1)}, bf16[128,1792]{1,0:T(8,128)(2,1)}, u32[]{:S(2)}, u32[]{:S(2)}) %collective-permute-start.1) | collective-permute-done | bytes 458784 | tf_op jit(solution)/shard_map/while/body/eval_jaxpr/ppermute | solution.py:13
  434.2 8.6 %collective-permute-done.1 = bf16[128,1792]{1,0:T(8,128)(2,1)} collective-permute-done((bf16[128,1792]{1,0:T(8,128)(2,1)S(1)}, bf16[128,1792]{1,0:T(8,128)(2,1)}, u32[]{:S(2)}, u32[]{:S(2)}) %collective-permute-start.1) | collective-permute-done | bytes 458784 | tf_op jit(solution)/shard_map/while/body/eval_jaxpr/ppermute | solution.py:13
  447.8 8.6 %collective-permute-done.1 = bf16[128,1792]{1,0:T(8,128)(2,1)} collective-permute-done((bf16[128,1792]{1,0:T(8,128)(2,1)S(1)}, bf16[128,1792]{1,0:T(8,128)(2,1)}, u32[]{:S(2)}, u32[]{:S(2)}) %collective-permute-start.1) | collective-permute-done | bytes 458784 | tf_op jit(solution)/shard_map/while/body/eval_jaxpr/ppermute | solution.py:13
  458.3 19.2 %psum.22 = f32[1792]{0:T(1024)S(1)} all-reduce(f32[1792]{0:T(1024)S(1)} %get-tuple-element.289), channel_id=1, replica_groups=mesh['tm'=8,'mp'=4,'tok'=8] {'tm'}, use_global_device_ids=true, to_apply=%region_6.7 | all-reduce | flops 1792 | bytes 14336 | tf_op jit(solution)/shard_map/psum | solution.py:66
  477.5 31.6 %psum.23 = f32[1792]{0:T(1024)} all-reduce(f32[1792]{0:T(1024)S(1)} %psum.22), channel_id=1, replica_groups=mesh['tm'=8,'mp'=4,'tok'=8] {'tok'}, use_global_device_ids=true, to_apply=%region_7.8 | all-reduce | flops 1792 | bytes 14336 | tf_op jit(solution)/shard_map/psum | solution.py:66
  (54 shorter events, 53.0 us)
Async XLA Ops:
  7.2 140.9 %all-gather.2.cloned.1.call-start = ((), (), s32[]{:S(2)}) async-start(), calls=%async_computation | async-start | bytes 13045760 | tf_op jit(solution)/shard_map/all_gather | solution.py:23
  7.9 343.2 %all-reduce.2.cloned.1.call-start = ((), (), s32[]{:S(2)}) async-start(), calls=%async_computation.1 | async-start | bytes 1835008 | tf_op jit(solution)/shard_map/psum | solution.py:48
  8.0 147.5 %copy-start.2 = (f32[1792]{0:T(1024)S(1)}, f32[1792]{0:T(1024)}, u32[]{:S(2)}) copy-start(f32[1792]{0:T(1024)} %param.11) | copy-start | bytes 21508
  157.1 4.5 collective-permute-start
  163.1 13.8 %collective-permute-start = (f32[128,1792]{1,0:T(8,128)}, f32[128,1792]{1,0:T(8,128)S(1)}, u32[]{:S(2)}, u32[]{:S(2)}) collective-permute-start(f32[128,1792]{1,0:T(8,128)} %get-tuple-element.455), channel_id=1, source_target_pairs={{0,32},{32,64},{64,96},{96,128},{128,160},{160,192},{192,224},{1,3... | collective-permute-start | bytes 2752520 | tf_op jit(solution)/shard_map/while/body/eval_jaxpr/ppermute | solution.py:13
  178.4 14.9 %collective-permute-start = (f32[128,1792]{1,0:T(8,128)}, f32[128,1792]{1,0:T(8,128)S(1)}, u32[]{:S(2)}, u32[]{:S(2)}) collective-permute-start(f32[128,1792]{1,0:T(8,128)} %get-tuple-element.455), channel_id=1, source_target_pairs={{0,32},{32,64},{64,96},{96,128},{128,160},{160,192},{192,224},{1,3... | collective-permute-start | bytes 2752520 | tf_op jit(solution)/shard_map/while/body/eval_jaxpr/ppermute | solution.py:13
  194.9 14.9 %collective-permute-start = (f32[128,1792]{1,0:T(8,128)}, f32[128,1792]{1,0:T(8,128)S(1)}, u32[]{:S(2)}, u32[]{:S(2)}) collective-permute-start(f32[128,1792]{1,0:T(8,128)} %get-tuple-element.455), channel_id=1, source_target_pairs={{0,32},{32,64},{64,96},{96,128},{128,160},{160,192},{192,224},{1,3... | collective-permute-start | bytes 2752520 | tf_op jit(solution)/shard_map/while/body/eval_jaxpr/ppermute | solution.py:13
  211.4 14.9 %collective-permute-start = (f32[128,1792]{1,0:T(8,128)}, f32[128,1792]{1,0:T(8,128)S(1)}, u32[]{:S(2)}, u32[]{:S(2)}) collective-permute-start(f32[128,1792]{1,0:T(8,128)} %get-tuple-element.455), channel_id=1, source_target_pairs={{0,32},{32,64},{64,96},{96,128},{128,160},{160,192},{192,224},{1,3... | collective-permute-start | bytes 2752520 | tf_op jit(solution)/shard_map/while/body/eval_jaxpr/ppermute | solution.py:13
  227.8 14.9 %collective-permute-start = (f32[128,1792]{1,0:T(8,128)}, f32[128,1792]{1,0:T(8,128)S(1)}, u32[]{:S(2)}, u32[]{:S(2)}) collective-permute-start(f32[128,1792]{1,0:T(8,128)} %get-tuple-element.455), channel_id=1, source_target_pairs={{0,32},{32,64},{64,96},{96,128},{128,160},{160,192},{192,224},{1,3... | collective-permute-start | bytes 2752520 | tf_op jit(solution)/shard_map/while/body/eval_jaxpr/ppermute | solution.py:13
  244.3 14.9 %collective-permute-start = (f32[128,1792]{1,0:T(8,128)}, f32[128,1792]{1,0:T(8,128)S(1)}, u32[]{:S(2)}, u32[]{:S(2)}) collective-permute-start(f32[128,1792]{1,0:T(8,128)} %get-tuple-element.455), channel_id=1, source_target_pairs={{0,32},{32,64},{64,96},{96,128},{128,160},{160,192},{192,224},{1,3... | collective-permute-start | bytes 2752520 | tf_op jit(solution)/shard_map/while/body/eval_jaxpr/ppermute | solution.py:13
  260.7 14.9 %collective-permute-start = (f32[128,1792]{1,0:T(8,128)}, f32[128,1792]{1,0:T(8,128)S(1)}, u32[]{:S(2)}, u32[]{:S(2)}) collective-permute-start(f32[128,1792]{1,0:T(8,128)} %get-tuple-element.455), channel_id=1, source_target_pairs={{0,32},{32,64},{64,96},{96,128},{128,160},{160,192},{192,224},{1,3... | collective-permute-start | bytes 2752520 | tf_op jit(solution)/shard_map/while/body/eval_jaxpr/ppermute | solution.py:13
  275.6 1.0 copy-start
  276.7 82.8 %copy-start.1 = (f32[128,1792]{1,0:T(8,128)S(1)}, f32[128,1792]{1,0:T(8,128)}, u32[]{:S(2)}) copy-start(f32[128,1792]{1,0:T(8,128)} %copy-done) | copy-start | bytes 2752516
  360.0 3.8 collective-permute-start.1
  367.5 7.2 %collective-permute-start.1 = (bf16[128,1792]{1,0:T(8,128)(2,1)S(1)}, bf16[128,1792]{1,0:T(8,128)(2,1)}, u32[]{:S(2)}, u32[]{:S(2)}) collective-permute-start(bf16[128,1792]{1,0:T(8,128)(2,1)S(1)} %get-tuple-element.465), channel_id=1, source_target_pairs={{32,0},{64,32},{96,64},{128,96},{160,128},{192,160},{224,192},{33,... | collective-permute-start | bytes 1376264 | tf_op jit(solution)/shard_map/while/body/eval_jaxpr/ppermute | solution.py:13
  378.4 9.9 %collective-permute-start.1 = (bf16[128,1792]{1,0:T(8,128)(2,1)S(1)}, bf16[128,1792]{1,0:T(8,128)(2,1)}, u32[]{:S(2)}, u32[]{:S(2)}) collective-permute-start(bf16[128,1792]{1,0:T(8,128)(2,1)S(1)} %get-tuple-element.465), channel_id=1, source_target_pairs={{32,0},{64,32},{96,64},{128,96},{160,128},{192,160},{224,192},{33,... | collective-permute-start | bytes 1376264 | tf_op jit(solution)/shard_map/while/body/eval_jaxpr/ppermute | solution.py:13
  392.0 9.9 %collective-permute-start.1 = (bf16[128,1792]{1,0:T(8,128)(2,1)S(1)}, bf16[128,1792]{1,0:T(8,128)(2,1)}, u32[]{:S(2)}, u32[]{:S(2)}) collective-permute-start(bf16[128,1792]{1,0:T(8,128)(2,1)S(1)} %get-tuple-element.465), channel_id=1, source_target_pairs={{32,0},{64,32},{96,64},{128,96},{160,128},{192,160},{224,192},{33,... | collective-permute-start | bytes 1376264 | tf_op jit(solution)/shard_map/while/body/eval_jaxpr/ppermute | solution.py:13
  405.6 9.9 %collective-permute-start.1 = (bf16[128,1792]{1,0:T(8,128)(2,1)S(1)}, bf16[128,1792]{1,0:T(8,128)(2,1)}, u32[]{:S(2)}, u32[]{:S(2)}) collective-permute-start(bf16[128,1792]{1,0:T(8,128)(2,1)S(1)} %get-tuple-element.465), channel_id=1, source_target_pairs={{32,0},{64,32},{96,64},{128,96},{160,128},{192,160},{224,192},{33,... | collective-permute-start | bytes 1376264 | tf_op jit(solution)/shard_map/while/body/eval_jaxpr/ppermute | solution.py:13
  419.2 9.9 %collective-permute-start.1 = (bf16[128,1792]{1,0:T(8,128)(2,1)S(1)}, bf16[128,1792]{1,0:T(8,128)(2,1)}, u32[]{:S(2)}, u32[]{:S(2)}) collective-permute-start(bf16[128,1792]{1,0:T(8,128)(2,1)S(1)} %get-tuple-element.465), channel_id=1, source_target_pairs={{32,0},{64,32},{96,64},{128,96},{160,128},{192,160},{224,192},{33,... | collective-permute-start | bytes 1376264 | tf_op jit(solution)/shard_map/while/body/eval_jaxpr/ppermute | solution.py:13
  432.8 9.9 %collective-permute-start.1 = (bf16[128,1792]{1,0:T(8,128)(2,1)S(1)}, bf16[128,1792]{1,0:T(8,128)(2,1)}, u32[]{:S(2)}, u32[]{:S(2)}) collective-permute-start(bf16[128,1792]{1,0:T(8,128)(2,1)S(1)} %get-tuple-element.465), channel_id=1, source_target_pairs={{32,0},{64,32},{96,64},{128,96},{160,128},{192,160},{224,192},{33,... | collective-permute-start | bytes 1376264 | tf_op jit(solution)/shard_map/while/body/eval_jaxpr/ppermute | solution.py:13
  446.4 9.9 %collective-permute-start.1 = (bf16[128,1792]{1,0:T(8,128)(2,1)S(1)}, bf16[128,1792]{1,0:T(8,128)(2,1)}, u32[]{:S(2)}, u32[]{:S(2)}) collective-permute-start(bf16[128,1792]{1,0:T(8,128)(2,1)S(1)} %get-tuple-element.465), channel_id=1, source_target_pairs={{32,0},{64,32},{96,64},{128,96},{160,128},{192,160},{224,192},{33,... | collective-permute-start | bytes 1376264 | tf_op jit(solution)/shard_map/while/body/eval_jaxpr/ppermute | solution.py:13
Sparse Core Ops, SparseCore 0:
  11.7 136.3 all-gather.1
  276.8 74.2 all-reduce.1
